TPU v7x, 256 devices: a whole 4x4x8 slice. The times are simulated.
256 devices in a mesh: blk: 16 (over x_lo, z), beam: 2 (over x_hi), head: 8 (over y, core).
Axes of the slice: x: 4 (x_hi: 2, x_lo: 2; x = x_hi * 2 + x_lo), y: 4, z: 8, core: 2. Of those that a mesh axis runs over, the one named last changes fastest.
Arguments:
- hidden_in: float32 [2, 512, 4096], P(None, 'beam', 'blk'), may hold values from -41 to 41
- norm_gains: float32 [2, 4096], P(None, 'blk'), may hold values from 0.1 to 1.9
- w_qkv: bfloat16 [4096, 3, 4096], P('blk', None, 'head'), may hold values from -0.09375 to 0.09375
- w_self_out: bfloat16 [4096, 4096], P('head', 'blk'), may hold values from -0.09375 to 0.09375
- w_cross_q: bfloat16 [4096, 4096], P('blk', 'head'), may hold values from -0.09375 to 0.09375
- w_cross_out: bfloat16 [4096, 4096], P('head', 'blk'), may hold values from -0.09375 to 0.09375
- pos_bias: float32 [64, 8], P('head'), may hold values from -4 to 4
- self_cache: bfloat16 [2, 2, 256, 6, 4096], P(None, 'beam', 'blk', None, 'head'), may hold values from -300 to 300
- memory: bfloat16 [2, 2048, 4096], P(None, 'blk', 'head'), may hold values from -300 to 300
- parents: int32 [2, 512], replicated, may hold values from 0 to 511, as said below
Outputs:
- hidden_out: float32 [2, 512, 4096], P(None, 'beam', 'blk')
- cache_out: bfloat16 [2, 2, 256, 8, 4096], P(None, 'beam', 'blk', None, 'head')
Inputs may be any that keep to these rules, and one draw needn't show every extreme that they name: In every step each aligned block of 16 rows takes at most 2 of its parents from any one aligned block of 16 rows, and exactly 2 from at least one.
All inputs are finite; a program needn't handle non-finite values.
Results may differ from a plain program's by a relative error of at most 0.022.
Values may be sent and summed in bfloat16 or wider, within the bound.
A program may use at most 128 MiB of HBM per device.

v0:
```python
import jax
import jax.numpy as jnp
from jax import lax
from jax.sharding import PartitionSpec as P

D = 4096
HEAD_DIM = 64
EPS = 1e-06


def combined_all(value, axis, join):
    gathered = jax.tree.map(
        lambda a, kind: lax.all_gather(a.astype(kind), axis),
        value,
        (jnp.bfloat16, jnp.bfloat16, jnp.bfloat16),
    )

    def take(source):
        return jax.tree.map(
            lambda a, own: lax.dynamic_index_in_dim(a, source, 0, False).astype(own.dtype),
            gathered,
            value,
        )

    return lax.fori_loop(
        1, lax.axis_size(axis), lambda source, state: join(state, take(source)), take(0)
    )


def project(states, norm_gain, weight):
    normed = (states * norm_gain).astype(jnp.bfloat16)
    partial_sum = jnp.dot(normed, weight, preferred_element_type=jnp.float32)
    squares = jnp.sum(states * states, axis=1)
    summed, square_sum = lax.psum((partial_sum, squares), "blk")
    inverse_rms = lax.rsqrt(square_sum / D + EPS)
    return (summed * inverse_rms[:, None]).astype(jnp.bfloat16)


def head_total(partial_sum):
    return lax.psum(partial_sum.astype(jnp.bfloat16), "head").astype(jnp.float32)


def routing(parent_list, block_rows, capacity):
    blk_count = lax.axis_size("blk")
    beam_count = lax.axis_size("beam")
    groups = blk_count * beam_count
    blocks = parent_list.reshape(groups, block_rows)
    source_block = blocks // block_rows
    source_dev = source_block % blk_count * beam_count + source_block // blk_count
    local_row = blocks % block_rows
    matching = source_dev[:, :, None] == source_dev[:, None, :]
    ordering = jnp.arange(block_rows, dtype=jnp.int32)
    earlier = ordering[None, :] < ordering[:, None]
    slot_index = jnp.sum((matching & earlier[None]).astype(jnp.int32), axis=2)
    self_index = lax.axis_index("blk") * beam_count + lax.axis_index("beam")
    owned_rows = source_dev == self_index
    selected = owned_rows[:, :, None] & (
        slot_index[:, :, None] == jnp.arange(capacity, dtype=jnp.int32)[None, None, :]
    )
    send_rows = jnp.sum(selected.astype(jnp.int32) * local_row[:, :, None], axis=1)
    send_rows = (
        send_rows.reshape(beam_count, blk_count, capacity)
        .transpose(1, 0, 2)
        .reshape(groups * capacity)
    )
    own_block = lax.axis_index("beam") * blk_count + lax.axis_index("blk")
    own_source = lax.dynamic_index_in_dim(source_dev, own_block, 0, keepdims=False)
    own_slot = lax.dynamic_index_in_dim(slot_index, own_block, 0, keepdims=False)
    return (send_rows, own_source * capacity + own_slot)


def reorder(cache_block, parent_list, capacity):
    send_rows, recv_rows = routing(parent_list, cache_block.shape[1], capacity)
    outgoing = jnp.take(cache_block, send_rows, axis=1)
    arrived = lax.all_to_all(outgoing, ("blk", "beam"), split_axis=1, concat_axis=1, tiled=True)
    return jnp.take(arrived, recv_rows, axis=1)


def self_attend(queries, grown_cache, position_bias):
    rows_here = grown_cache.shape[1]
    length = grown_cache.shape[2]
    heads_here = position_bias.shape[0]
    split_queries = queries.reshape(rows_here, heads_here, HEAD_DIM)
    key_part = grown_cache[0].reshape(rows_here, length, heads_here, HEAD_DIM)
    value_part = grown_cache[1].reshape(rows_here, length, heads_here, HEAD_DIM)
    scores = (
        jnp.einsum("rhd,rjhd->rhj", split_queries, key_part, preferred_element_type=jnp.float32)
        * HEAD_DIM ** (-0.5)
        + position_bias[None]
    )
    maxima = jnp.max(scores, axis=2, keepdims=True)
    weights = jnp.exp(scores - maxima)
    totals = jnp.sum(weights, axis=2)
    mixed = jnp.einsum(
        "rhj,rjhd->rhd",
        weights.astype(jnp.bfloat16),
        value_part,
        preferred_element_type=jnp.float32,
    )
    mixed = mixed / totals[:, :, None]
    return mixed.reshape(rows_here, heads_here * HEAD_DIM).astype(jnp.bfloat16)


def cross_block(queries, memory):
    rows_here = queries.shape[0]
    heads_here = queries.shape[1] // HEAD_DIM
    split_queries = queries.reshape(rows_here, heads_here, HEAD_DIM)
    key_part = memory[0].reshape(-1, heads_here, HEAD_DIM)
    value_part = memory[1].reshape(-1, heads_here, HEAD_DIM)
    scores = jnp.einsum(
        "rhd,ehd->rhe", split_queries, key_part, preferred_element_type=jnp.float32
    ) * HEAD_DIM ** (-0.5)
    maxima = jnp.max(scores, axis=2)
    weights = jnp.exp(scores - maxima[:, :, None])
    totals = jnp.sum(weights, axis=2)
    accumulated = jnp.einsum(
        "rhe,ehd->rhd", weights.astype(jnp.bfloat16), value_part, preferred_element_type=jnp.float32
    )
    return (accumulated.reshape(rows_here, heads_here * HEAD_DIM), maxima, totals)


def cross_partial(queries, memory):
    rows_here = queries.shape[0]
    blocked = queries.reshape(rows_here // rows_here, rows_here, queries.shape[1])

    def one_block(query_block):
        return cross_block(query_block, memory)

    accumulated, maxima, totals = lax.map(one_block, blocked)
    return (
        accumulated.reshape(rows_here, -1),
        maxima.reshape(rows_here, -1),
        totals.reshape(rows_here, -1),
    )


def combine_parts(earlier_part, later_part):
    accum_first, peak_first, total_first = earlier_part
    accum_second, peak_second, total_second = later_part
    joint_max = jnp.maximum(peak_first, peak_second)
    factor_first = jnp.exp(peak_first - joint_max)
    factor_second = jnp.exp(peak_second - joint_max)
    rows_here, heads_here = peak_first.shape
    scaled_first = accum_first.reshape(rows_here, heads_here, -1) * factor_first[:, :, None]
    scaled_second = accum_second.reshape(rows_here, heads_here, -1) * factor_second[:, :, None]
    joined = (scaled_first + scaled_second).reshape(accum_first.shape)
    return (joined, joint_max, total_first * factor_first + total_second * factor_second)


def body(
    hidden_in,
    norm_gains,
    w_qkv,
    w_self_out,
    w_cross_q,
    w_cross_out,
    pos_bias,
    self_cache,
    memory,
    parents,
):
    blk_count = lax.axis_size("blk")
    beam_count = lax.axis_size("beam")
    block_rows = self_cache.shape[2]
    capacity = max(2, -(-block_rows // (blk_count * beam_count)))
    united_qkv = w_qkv.reshape(w_qkv.shape[0], -1)
    inner_here = w_cross_q.shape[1]
    first_row = lax.axis_index("blk") * block_rows
    steps_total = hidden_in.shape[0]
    held_cache = reorder(self_cache[:, 0], parents[0], capacity)
    outputs = []
    for step_index in range(steps_total):
        following = step_index + 1 < steps_total
        states = hidden_in[step_index]
        fresh_qkv = project(states, norm_gains[0], united_qkv)
        own_qkv = lax.dynamic_slice_in_dim(fresh_qkv, first_row, block_rows, 0).reshape(
            block_rows, 3, inner_here
        )
        fresh_entry = jnp.stack([own_qkv[:, 1], own_qkv[:, 2]])[:, :, None]
        grown_cache = jnp.concatenate([held_cache, fresh_entry], axis=2)
        length = grown_cache.shape[2]
        position_bias = jnp.flip(pos_bias[:, :length], axis=1)
        attended = self_attend(own_qkv[:, 0], grown_cache, position_bias)
        projected = jnp.dot(
            lax.all_gather(attended, "blk", axis=0, tiled=True),
            w_self_out,
            preferred_element_type=jnp.float32,
        )
        middle = states + head_total(projected)
        cross_query = project(middle, norm_gains[1], w_cross_q)
        accumulated, peak_scores, totals = cross_partial(cross_query, memory)
        accumulated, peak_scores, totals = combined_all(
            (accumulated, peak_scores, totals), "blk", combine_parts
        )
        rows_here, heads_here = totals.shape
        cross_mixed = (
            (accumulated.reshape(rows_here, heads_here, -1) / totals[:, :, None])
            .reshape(rows_here, -1)
            .astype(jnp.bfloat16)
        )
        outputs.append(
            middle
            + head_total(jnp.dot(cross_mixed, w_cross_out, preferred_element_type=jnp.float32))
        )
        if following:
            held_cache = reorder(grown_cache, parents[step_index + 1], capacity)
        else:
            held_cache = grown_cache
    return (jnp.stack(outputs), held_cache[:, None])


def solution(mesh):
    placed = (
        P(None, "beam", "blk"),
        P(None, "blk"),
        P("blk", None, "head"),
        P("head", "blk"),
        P("blk", "head"),
        P("head", "blk"),
        P("head", None),
        P(None, "beam", "blk", None, "head"),
        P(None, "blk", "head"),
        P(),
    )
    return jax.shard_map(
        body,
        mesh=mesh,
        in_specs=placed,
        out_specs=(P(None, "beam", "blk"), P(None, "beam", "blk", None, "head")),
        check_vma=False,
    )
```

profile of v0, /device:TPU:2, one launch (start us, length us, event | category | flops | bytes accessed | tf_op | source)
XLA Modules:
  0.0 719.9 jit_solution(7970170962780751000)
XLA Ops:
  9.4 1.5 fusion.42
  11.0 1.6 fusion.38
  14.8 2.1 gather_fusion
  17.0 1.7 fusion.16
  18.7 11.6 %all-to-all-start = ((bf16[2,64,6,512]{3,0,2,1:T(2,128)(2,1)}), bf16[2,64,6,512]{3,0,2,1:T(2,128)(2,1)S(1)}, u32[]{:S(2)}, u32[]{:S(2)}) async-start(bf16[2,64,6,512]{3,0,2,1:T(2,128)(2,1)} %fusion.16), calls=%async_computation | async-start | bytes 1572864 | tf_op jit(solution)/shard_map/all_to_all | solution.py:75
  30.6 53.1 %all-reduce.1 = (f32[256]{0:T(256)S(1)}, f32[256]{0:T(256)S(1)}) all-reduce(f32[256]{0:T(256)S(1)} %get-tuple-element.453, f32[256]{0:T(256)S(1)} %get-tuple-element.452), channel_id=1, replica_groups=mesh['blk'=16,'beam'=2,'head'=8] {'blk'}, use_global_device_ids=true, to_apply=%region_18.19 | all-reduce | flops 512 | bytes 4096 | tf_op jit(solution)/shard_map/psum | solution.py:34
  85.5 87.4 %all-reduce.13.cloned.1.call-done = (f32[256,1536]{1,0:T(8,128)}, f32[256,1536]{1,0:T(8,128)}) async-done(((f32[256,1536]{1,0:T(8,128)}, f32[256,1536]{1,0:T(8,128)}), (f32[256,1536]{1,0:T(8,128)}, f32[256,1536]{1,0:T(8,128)})) %all-reduce.13.cloned.1.call-update) | async-done | bytes 3145744 | tf_op jit(solution)/shard_map/psum | solution.py:34
  174.5 2.4 gather_fusion.2
  176.9 1.9 fusion.15
  178.8 8.1 %all-to-all-start.1 = ((bf16[2,64,7,512]{3,0,2,1:T(2,128)(2,1)}), bf16[2,64,7,512]{3,0,2,1:T(2,128)(2,1)S(1)}, u32[]{:S(2)}, u32[]{:S(2)}) async-start(bf16[2,64,7,512]{3,0,2,1:T(2,128)(2,1)} %fusion.15), calls=%async_computation.1 | async-start | bytes 1835008 | tf_op jit(solution)/shard_map/all_to_all | solution.py:75
  190.5 36.8 %all_gather.30 = bf16[256,512]{1,0:T(8,128)(2,1)S(1)} all-gather(bf16[16,512]{1,0:T(8,128)(2,1)S(1)} %convert_element_type.302), channel_id=1, replica_groups=mesh['blk'=16,'beam'=2,'head'=8] {'blk'}, dimensions={0}, use_global_device_ids=true | all-gather | bytes 278528 | tf_op jit(solution)/shard_map/all_gather | solution.py:185
  232.9 31.7 %all_gather.34 = bf16[256,512]{1,0:T(8,128)(2,1)S(1)} all-gather(bf16[16,512]{1,0:T(8,128)(2,1)S(1)} %convert_element_type.330), channel_id=1, replica_groups=mesh['blk'=16,'beam'=2,'head'=8] {'blk'}, dimensions={0}, use_global_device_ids=true | all-gather | bytes 278528 | tf_op jit(solution)/shard_map/all_gather | solution.py:185
  265.6 62.7 %all-reduce.17.cloned.1.call-done = (bf16[256,256]{1,0:T(8,128)(2,1)}, bf16[256,256]{1,0:T(8,128)(2,1)}) async-done(((bf16[256,256]{1,0:T(8,128)(2,1)}, bf16[256,256]{1,0:T(8,128)(2,1)}), (bf16[256,256]{1,0:T(8,128)(2,1)}, bf16[256,256]{1,0:T(8,128)(2,1)})) %all-reduce.17.cloned.1.call-update) | async-done | bytes 262160 | tf_op jit(solution)/shard_map/psum | solution.py:40
  328.4 2.0 fusion.44
  330.4 2.0 fusion.40
  332.9 33.9 %all-reduce = (f32[256]{0:T(256)S(1)}, f32[256]{0:T(256)S(1)}) all-reduce(f32[256]{0:T(256)S(1)} %get-tuple-element.451, f32[256]{0:T(256)S(1)} %get-tuple-element.450), channel_id=1, replica_groups=mesh['blk'=16,'beam'=2,'head'=8] {'blk'}, use_global_device_ids=true, to_apply=%region_26.27 | all-reduce | flops 512 | bytes 4096 | tf_op jit(solution)/shard_map/psum | solution.py:34
  366.8 101.9 %all-reduce.11.cloned.1.call-done = (f32[256,512]{1,0:T(8,128)}, f32[256,512]{1,0:T(8,128)}) async-done(((f32[256,512]{1,0:T(8,128)}, f32[256,512]{1,0:T(8,128)}), (f32[256,512]{1,0:T(8,128)}, f32[256,512]{1,0:T(8,128)})) %all-reduce.11.cloned.1.call-update) | async-done | bytes 1048592 | tf_op jit(solution)/shard_map/psum | solution.py:34
  473.5 32.7 %all-gather = bf16[4096,8]{0,1:T(8,128)(2,1)S(1)} all-gather(bf16[256,8]{0,1:T(8,128)(2,1)S(1)} %convert_element_type.313), channel_id=2, replica_groups=mesh['blk'=16,'beam'=2,'head'=8] {'blk'}, dimensions={0}, use_global_device_ids=true | all-gather | bytes 69632 | tf_op jit(solution)/shard_map/all_gather | solution.py:13
  506.3 29.9 %all-gather.1 = bf16[4096,8]{0,1:T(8,128)(2,1)S(1)} all-gather(bf16[256,8]{0,1:T(8,128)(2,1)S(1)} %fusion.11), channel_id=3, replica_groups=mesh['blk'=16,'beam'=2,'head'=8] {'blk'}, dimensions={0}, use_global_device_ids=true | all-gather | bytes 69632 | tf_op jit(solution)/shard_map/all_gather | solution.py:13
  536.2 31.8 %all-gather.2 = bf16[4096,8]{0,1:T(8,128)(2,1)S(1)} all-gather(bf16[256,8]{0,1:T(8,128)(2,1)S(1)} %convert_element_type.341), channel_id=4, replica_groups=mesh['blk'=16,'beam'=2,'head'=8] {'blk'}, dimensions={0}, use_global_device_ids=true | all-gather | bytes 69632 | tf_op jit(solution)/shard_map/all_gather | solution.py:13
  568.2 29.9 %all-gather.3 = bf16[4096,8]{0,1:T(8,128)(2,1)S(1)} all-gather(bf16[256,8]{0,1:T(8,128)(2,1)S(1)} %fusion.13), channel_id=5, replica_groups=mesh['blk'=16,'beam'=2,'head'=8] {'blk'}, dimensions={0}, use_global_device_ids=true | all-gather | bytes 69632 | tf_op jit(solution)/shard_map/all_gather | solution.py:13
  599.4 21.4 %while.24 = (s32[]{:T(128)}, f32[256,512]{0,1:T(8,128)S(1)}, f32[256,8]{0,1:T(8,128)S(1)}, f32[256,8]{0,1:T(8,128)S(1)}, bf16[16,256,8]{1,2,0:T(8,128)(2,1)S(1)}...) while((s32[]{:T(128)}, f32[256,512]{0,1:T(8,128)S(1)}, ...), condition=%wide.region_14.15_spmd, body=%wide.region_13.14_spmd.sunk | while | flops 540677 | bytes 2433167 | solution.py:25
  623.3 21.4 %while.25 = (s32[]{:T(128)}, f32[256,512]{0,1:T(8,128)S(1)}, f32[256,8]{0,1:T(8,128)S(1)}, f32[256,8]{0,1:T(8,128)S(1)}, bf16[16,256,8]{1,2,0:T(8,128)(2,1)S(1)}...) while((s32[]{:T(128)}, f32[256,512]{0,1:T(8,128)S(1)}, ...), condition=%wide.region_30.31_spmd, body=%wide.region_29.30_spmd.sunk | while | flops 540677 | bytes 2433167 | solution.py:25
  647.9 63.2 %all-reduce.15.cloned.1.call-done = (bf16[256,256]{1,0:T(8,128)(2,1)}, bf16[256,256]{1,0:T(8,128)(2,1)}) async-done(((bf16[256,256]{1,0:T(8,128)(2,1)}, bf16[256,256]{1,0:T(8,128)(2,1)}), (bf16[256,256]{1,0:T(8,128)(2,1)}, bf16[256,256]{1,0:T(8,128)(2,1)})) %all-reduce.15.cloned.1.call-update) | async-done | bytes 262160 | tf_op jit(solution)/shard_map/psum | solution.py:40
  (292 shorter events, 73.8 us)
Async XLA Ops:
  7.2 321.2 %copy-start = (bf16[256,512]{1,0:T(8,128)(2,1)S(1)}, bf16[256,512]{1,0:T(8,128)(2,1)}, u32[]{:S(2)}) copy-start(bf16[256,512]{1,0:T(8,128)(2,1)} %param.18) | copy-start | bytes 786436
  7.2 2.2 copy-start.1
  7.2 165.7 %all-reduce.13.cloned.1.call-start = ((), (), s32[]{:S(2)}) async-start(), calls=%async_computation.5 | async-start | bytes 6291456 | tf_op jit(solution)/shard_map/psum | solution.py:34
  12.5 0.7 copy-start.15
  12.6 2.0 copy-start.13
  18.7 65.6 %all-to-all-start = ((bf16[2,64,6,512]{3,0,2,1:T(2,128)(2,1)}), bf16[2,64,6,512]{3,0,2,1:T(2,128)(2,1)S(1)}, u32[]{:S(2)}, u32[]{:S(2)}) async-start(bf16[2,64,6,512]{3,0,2,1:T(2,128)(2,1)} %fusion.16), calls=%async_computation | async-start | bytes 1572864 | tf_op jit(solution)/shard_map/all_to_all | solution.py:75
  176.9 10.2 %copy-start.14 = (f32[8,8]{1,0:T(8,128)S(1)}, f32[8,8]{1,0:T(8,128)}, u32[]{:S(2)}) copy-start(f32[8,8]{1,0:T(8,128)} %param.20) | copy-start | bytes 772
  178.8 49.5 %all-to-all-start.1 = ((bf16[2,64,7,512]{3,0,2,1:T(2,128)(2,1)}), bf16[2,64,7,512]{3,0,2,1:T(2,128)(2,1)S(1)}, u32[]{:S(2)}, u32[]{:S(2)}) async-start(bf16[2,64,7,512]{3,0,2,1:T(2,128)(2,1)} %fusion.15), calls=%async_computation.1 | async-start | bytes 1835008 | tf_op jit(solution)/shard_map/all_to_all | solution.py:75
  186.9 141.5 %all-reduce.17.cloned.1.call-start = ((), (), s32[]{:S(2)}) async-start(), calls=%async_computation.7 | async-start | bytes 524288 | tf_op jit(solution)/shard_map/psum | solution.py:40
  187.6 39.8 %copy-start.7 = (bf16[512,256]{1,0:T(8,128)(2,1)S(1)}, bf16[512,256]{1,0:T(8,128)(2,1)}, u32[]{:S(2)}) copy-start(bf16[512,256]{1,0:T(8,128)(2,1)} %param.17) | copy-start | bytes 786436
  187.6 41.9 %copy-start.10 = (bf16[2,16,1,512]{3,0,2,1:T(2,128)(2,1)}, bf16[2,16,1,512]{3,0,2,1:T(2,128)(2,1)S(1)}, u32[]{:S(2)}) copy-start(bf16[2,16,1,512]{3,0,2,1:T(2,128)(2,1)S(1)} %copy.165) | copy-start | bytes 98308
  229.5 36.0 %copy-start.2 = (bf16[2,16,7,512]{3,0,2,1:T(2,128)(2,1)}, bf16[2,16,7,512]{3,0,2,1:T(2,128)(2,1)S(1)}, u32[]{:S(2)}) copy-start(bf16[2,16,7,512]{3,0,2,1:T(2,128)(2,1)S(1)} %fusion.35) | copy-start | bytes 688132
  265.6 203.1 %all-reduce.11.cloned.1.call-start = ((), (), s32[]{:S(2)}) async-start(), calls=%async_computation.4 | async-start | bytes 2097152 | tf_op jit(solution)/shard_map/psum | solution.py:34
  328.4 4.1 copy-start.12
  330.4 2.4 copy-start.4
  330.4 2.4 copy-start.5
  332.4 265.8 %all-gather.7.cloned.1.call-start = ((), (), s32[]{:S(2)}) async-start(), calls=%async_computation.2 | async-start | bytes 4456448 | tf_op jit(solution)/shard_map/all_gather | solution.py:13
  470.0 1.6 copy-start.9
  471.6 150.5 %all-gather.9.cloned.1.call-start = ((), (), s32[]{:S(2)}) async-start(), calls=%async_computation.3 | async-start | bytes 4456448 | tf_op jit(solution)/shard_map/all_gather | solution.py:13
  473.4 237.7 %all-reduce.15.cloned.1.call-start = ((), (), s32[]{:S(2)}) async-start(), calls=%async_computation.6 | async-start | bytes 524288 | tf_op jit(solution)/shard_map/psum | solution.py:40
  623.3 21.5 %copy-start.8 = (bf16[512,256]{1,0:T(8,128)(2,1)S(1)}, bf16[512,256]{1,0:T(8,128)(2,1)}, u32[]{:S(2)}) copy-start(bf16[512,256]{1,0:T(8,128)(2,1)} %param.19) | copy-start | bytes 786436
  644.8 2.0 copy-start.3
  644.8 2.0 copy-start.11
  644.8 66.3 %copy-start.6 = (bf16[256,256]{1,0:T(8,128)(2,1)S(1)}, bf16[256,256]{1,0:T(8,128)(2,1)}, u32[]{:S(2)}) copy-start(bf16[256,256]{1,0:T(8,128)(2,1)} %get-tuple-element.501) | copy-start | bytes 393220
Sparse Core Ops, SparseCore 0:
  12.7 160.1 all-reduce.12
  265.7 62.6 all-reduce.16
  332.5 136.1 all-reduce.10
  471.7 74.3 all-gather.6
  548.3 73.7 all-gather.8
  646.9 64.1 all-reduce.14
where the time goes:
time: 721 us; the launch traced here: 720 us
  waiting for transfers between devices  317 us (44%)
  blocking collectives  280 us (39%)
  local copies, waits for them, and re-layouts  49.8 us (7%)
  other arithmetic  24.3 us (3%)
  starting transfers between devices  20.1 us (3%)
  between operations  14.9 us (2%)
  matrix products  13.2 us (2%)
    psum x2, waiting for transfers between devices, project(): summed, square_sum = lax.psum((partial_sum, squares), 'blk')  189 us
    psum x2, waiting for transfers between devices, head_total(): lax.psum(partial_sum.astype(jnp.bfloat16), 'head').astype(jnp.float32)  126 us
    all_gather x4, blocking collectives, combined_all(): lax.all_gather(a.astype(kind), axis)  124 us
    psum x2, blocking collectives, project(): summed, square_sum = lax.psum((partial_sum, squares), 'blk')  87 us
    all_gather x2, blocking collectives, body(): lax.all_gather(attended, 'blk', axis=0, tiled=True)  68.6 us
    dynamic_slice x60, local copies, waits for them, and re-layouts, take(): lax.dynamic_index_in_dim(a, source, 0, False).astype(own.dtype)  33.3 us
    all_to_all x2, starting transfers between devices, reorder(): lax.all_to_all(outgoing, ('blk', 'beam'), split_axis=1, concat_axis=1, ti...  19.7 us
  transfers between devices with their start and end apart: 8, of which 5 were waited for; matrix products, arithmetic and copies ran while one was open for 5% of the time, Pallas kernels for 0%

commit v1 on v0

--- a/solution.py
+++ b/solution.py
@@ -37,7 +37,9 @@
 
 
 def head_total(partial_sum):
-    return lax.psum(partial_sum.astype(jnp.bfloat16), "head").astype(jnp.float32)
+    return jnp.sum(lax.all_gather(partial_sum.astype(jnp.bfloat16), "head"), axis=0).astype(
+        jnp.float32
+    )
 
 
 def routing(parent_list, block_rows, capacity):

time: 721 us -> 666 us (0.924)
  waiting for transfers between devices: 317 us -> 232 us
  other arithmetic: 24.3 us -> 49.3 us
    psum x2 -> x0, waiting for transfers between devices: 126 us -> none  [head_total(): lax.psum(partial_sum.astype(jnp.bfloat16), 'head').astype(jnp.float32)]
    all_gather x0 -> x4, waiting for transfers between devices: none -> 42.6 us  [head_total(): lax.all_gather(partial_sum.astype(jnp.bfloat16), 'head')]
    add x30, other arithmetic: 0.6 us -> 21.1 us  [combine_parts(): total_first * factor_first + total_second * factor_second]
  transfers between devices with their start and end apart: 8 -> 10, of which waited for: 5 -> 4; matrix products, arithmetic and copies ran while one was open for 5% -> 14% of each run, Pallas kernels for 0% -> 0%
where the time goes in v1:
time: 666 us; the launch traced here: 662 us
  blocking collectives  280 us (42%)
  waiting for transfers between devices  232 us (35%)
  local copies, waits for them, and re-layouts  51.4 us (8%)
  other arithmetic  49.3 us (7%)
  starting transfers between devices  20.2 us (3%)
  between operations  14.9 us (2%)
  matrix products  12.9 us (2%)
    psum x2, waiting for transfers between devices, project(): summed, square_sum = lax.psum((partial_sum, squares), 'blk')  189 us
    all_gather x4, blocking collectives, combined_all(): lax.all_gather(a.astype(kind), axis)  124 us
    psum x2, blocking collectives, project(): summed, square_sum = lax.psum((partial_sum, squares), 'blk')  87.1 us
    all_gather x2, blocking collectives, body(): lax.all_gather(attended, 'blk', axis=0, tiled=True)  68.8 us
    all_gather x4, waiting for transfers between devices, head_total(): lax.all_gather(partial_sum.astype(jnp.bfloat16), 'head')  42.6 us
    dynamic_slice x60, local copies, waits for them, and re-layouts, take(): lax.dynamic_index_in_dim(a, source, 0, False).astype(own.dtype)  33.3 us
    add x30, other arithmetic, combine_parts(): total_first * factor_first + total_second * factor_second  21.1 us
    all_to_all x2, starting transfers between devices, reorder(): lax.all_to_all(outgoing, ('blk', 'beam'), split_axis=1, concat_axis=1, ti...  19.7 us
  transfers between devices with their start and end apart: 10, of which 4 were waited for; matrix products, arithmetic and copies ran while one was open for 14% of the time, Pallas kernels for 0%

profile of v1, /device:TPU:2, one launch (start us, length us, event | category | flops | bytes accessed | tf_op | source)
XLA Modules:
  0.0 662.0 jit_solution(9248153029548785351)
XLA Ops:
  9.4 1.5 fusion.46
  11.0 1.6 fusion.42
  14.8 2.1 gather_fusion
  16.9 1.7 fusion.16
  18.6 11.6 %all-to-all-start = ((bf16[2,64,6,512]{3,0,2,1:T(2,128)(2,1)}), bf16[2,64,6,512]{3,0,2,1:T(2,128)(2,1)S(1)}, u32[]{:S(2)}, u32[]{:S(2)}) async-start(bf16[2,64,6,512]{3,0,2,1:T(2,128)(2,1)} %fusion.16), calls=%async_computation | async-start | bytes 1572864 | tf_op jit(solution)/shard_map/all_to_all | solution.py:77
  30.6 53.1 %all-reduce.1 = (f32[256]{0:T(256)S(1)}, f32[256]{0:T(256)S(1)}) all-reduce(f32[256]{0:T(256)S(1)} %get-tuple-element.453, f32[256]{0:T(256)S(1)} %get-tuple-element.452), channel_id=1, replica_groups=mesh['blk'=16,'beam'=2,'head'=8] {'blk'}, use_global_device_ids=true, to_apply=%region_18.19 | all-reduce | flops 512 | bytes 4096 | tf_op jit(solution)/shard_map/psum | solution.py:34
  85.5 86.3 %all-reduce.9.cloned.1.call-done = (f32[256,1536]{1,0:T(8,128)}, f32[256,1536]{1,0:T(8,128)}) async-done(((f32[256,1536]{1,0:T(8,128)}, f32[256,1536]{1,0:T(8,128)}), (f32[256,1536]{1,0:T(8,128)}, f32[256,1536]{1,0:T(8,128)})) %all-reduce.9.cloned.1.call-update) | async-done | bytes 3145744 | tf_op jit(solution)/shard_map/psum | solution.py:34
  173.4 2.4 gather_fusion.2
  175.8 1.9 fusion.15
  177.7 8.1 %all-to-all-start.1 = ((bf16[2,64,7,512]{3,0,2,1:T(2,128)(2,1)}), bf16[2,64,7,512]{3,0,2,1:T(2,128)(2,1)S(1)}, u32[]{:S(2)}, u32[]{:S(2)}) async-start(bf16[2,64,7,512]{3,0,2,1:T(2,128)(2,1)} %fusion.15), calls=%async_computation.1 | async-start | bytes 1835008 | tf_op jit(solution)/shard_map/all_to_all | solution.py:77
  189.3 37.0 %all_gather.54 = bf16[256,512]{1,0:T(8,128)(2,1)S(1)} all-gather(bf16[16,512]{1,0:T(8,128)(2,1)S(1)} %convert_element_type.354), channel_id=1, replica_groups=mesh['blk'=16,'beam'=2,'head'=8] {'blk'}, dimensions={0}, use_global_device_ids=true | all-gather | bytes 278528 | tf_op jit(solution)/shard_map/all_gather | solution.py:187
  232.1 31.8 %all_gather.62 = bf16[256,512]{1,0:T(8,128)(2,1)S(1)} all-gather(bf16[16,512]{1,0:T(8,128)(2,1)S(1)} %convert_element_type.385), channel_id=1, replica_groups=mesh['blk'=16,'beam'=2,'head'=8] {'blk'}, dimensions={0}, use_global_device_ids=true | all-gather | bytes 278528 | tf_op jit(solution)/shard_map/all_gather | solution.py:187
  267.3 21.0 %all-gather.23.cloned.1.call-done = bf16[2048,256]{1,0:T(8,128)(2,1)} async-done(((bf16[256,256]{1,0:T(8,128)(2,1)}), bf16[2048,256]{1,0:T(8,128)(2,1)}) %all-gather.23.cloned.1.call-update) | async-done | bytes 1048592 | tf_op jit(solution)/shard_map/all_gather | solution.py:40
  288.3 1.4 reduce_sum.170
  291.3 34.0 %all-reduce = (f32[256]{0:T(256)S(1)}, f32[256]{0:T(256)S(1)}) all-reduce(f32[256]{0:T(256)S(1)} %get-tuple-element.451, f32[256]{0:T(256)S(1)} %get-tuple-element.450), channel_id=1, replica_groups=mesh['blk'=16,'beam'=2,'head'=8] {'blk'}, use_global_device_ids=true, to_apply=%region_26.27 | all-reduce | flops 512 | bytes 4096 | tf_op jit(solution)/shard_map/psum | solution.py:34
  325.3 102.8 %all-reduce.7.cloned.1.call-done = (f32[256,512]{1,0:T(8,128)}, f32[256,512]{1,0:T(8,128)}) async-done(((f32[256,512]{1,0:T(8,128)}, f32[256,512]{1,0:T(8,128)}), (f32[256,512]{1,0:T(8,128)}, f32[256,512]{1,0:T(8,128)})) %all-reduce.7.cloned.1.call-update) | async-done | bytes 1048592 | tf_op jit(solution)/shard_map/psum | solution.py:34
  434.3 1.8 copy.169
  436.2 32.7 %all-gather.1 = bf16[4096,8]{0,1:T(8,128)(2,1)S(1)} all-gather(bf16[256,8]{0,1:T(8,128)(2,1)S(1)} %convert_element_type.367), channel_id=3, replica_groups=mesh['blk'=16,'beam'=2,'head'=8] {'blk'}, dimensions={0}, use_global_device_ids=true | all-gather | bytes 69632 | tf_op jit(solution)/shard_map/all_gather | solution.py:13
  469.1 30.0 %all-gather.2 = bf16[4096,8]{0,1:T(8,128)(2,1)S(1)} all-gather(bf16[256,8]{0,1:T(8,128)(2,1)S(1)} %fusion.11), channel_id=4, replica_groups=mesh['blk'=16,'beam'=2,'head'=8] {'blk'}, dimensions={0}, use_global_device_ids=true | all-gather | bytes 69632 | tf_op jit(solution)/shard_map/all_gather | solution.py:13
  499.1 31.8 %all-gather.5 = bf16[4096,8]{0,1:T(8,128)(2,1)S(1)} all-gather(bf16[256,8]{0,1:T(8,128)(2,1)S(1)} %convert_element_type.398), channel_id=7, replica_groups=mesh['blk'=16,'beam'=2,'head'=8] {'blk'}, dimensions={0}, use_global_device_ids=true | all-gather | bytes 69632 | tf_op jit(solution)/shard_map/all_gather | solution.py:13
  531.0 30.0 %all-gather.6 = bf16[4096,8]{0,1:T(8,128)(2,1)S(1)} all-gather(bf16[256,8]{0,1:T(8,128)(2,1)S(1)} %fusion.13), channel_id=8, replica_groups=mesh['blk'=16,'beam'=2,'head'=8] {'blk'}, dimensions={0}, use_global_device_ids=true | all-gather | bytes 69632 | tf_op jit(solution)/shard_map/all_gather | solution.py:13
  562.3 31.7 %while.24 = (s32[]{:T(128)}, f32[256,512]{0,1:T(8,128)S(1)}, f32[256,8]{0,1:T(8,128)S(1)}, f32[256,8]{0,1:T(8,128)S(1)}, bf16[16,256,8]{1,2,0:T(8,128)(2,1)}, /*...) while((s32[]{:T(128)}, f32[256,512]{0,1:T(8,128)S(1)}, ...), condition=%wide.region_14.15_spmd, body=%wide.region_13.14_spmd.sunk | while | flops 540677 | bytes 2433167 | solution.py:25
  596.3 31.5 %while.25 = (s32[]{:T(128)}, f32[256,512]{0,1:T(8,128)S(1)}, f32[256,8]{0,1:T(8,128)S(1)}, f32[256,8]{0,1:T(8,128)S(1)}, bf16[16,256,8]{1,2,0:T(8,128)(2,1)}, /*...) while((s32[]{:T(128)}, f32[256,512]{0,1:T(8,128)S(1)}, ...), condition=%wide.region_30.31_spmd, body=%wide.region_29.30_spmd.sunk | while | flops 540677 | bytes 2433167 | solution.py:25
  631.3 21.6 %all-gather.25.cloned.1.call-done = bf16[2048,256]{1,0:T(8,128)(2,1)} async-done(((bf16[256,256]{1,0:T(8,128)(2,1)}), bf16[2048,256]{1,0:T(8,128)(2,1)}) %all-gather.25.cloned.1.call-update) | async-done | bytes 1048592 | tf_op jit(solution)/shard_map/all_gather | solution.py:40
  (296 shorter events, 99.9 us)
Async XLA Ops:
  7.2 259.1 %copy-start = (bf16[256,512]{1,0:T(8,128)(2,1)S(1)}, bf16[256,512]{1,0:T(8,128)(2,1)}, u32[]{:S(2)}) copy-start(bf16[256,512]{1,0:T(8,128)(2,1)} %param.18) | copy-start | bytes 786436
  7.2 2.2 copy-start.1
  7.2 164.6 %all-reduce.9.cloned.1.call-start = ((), (), s32[]{:S(2)}) async-start(), calls=%async_computation.9 | async-start | bytes 6291456 | tf_op jit(solution)/shard_map/psum | solution.py:34
  12.5 0.7 copy-start.12
  12.5 2.0 copy-start.7
  18.6 65.6 %all-to-all-start = ((bf16[2,64,6,512]{3,0,2,1:T(2,128)(2,1)}), bf16[2,64,6,512]{3,0,2,1:T(2,128)(2,1)S(1)}, u32[]{:S(2)}, u32[]{:S(2)}) async-start(bf16[2,64,6,512]{3,0,2,1:T(2,128)(2,1)} %fusion.16), calls=%async_computation | async-start | bytes 1572864 | tf_op jit(solution)/shard_map/all_to_all | solution.py:77
  175.8 10.2 %copy-start.11 = (f32[8,8]{1,0:T(8,128)S(1)}, f32[8,8]{1,0:T(8,128)}, u32[]{:S(2)}) copy-start(f32[8,8]{1,0:T(8,128)} %param.20) | copy-start | bytes 772
  177.7 49.7 %all-to-all-start.1 = ((bf16[2,64,7,512]{3,0,2,1:T(2,128)(2,1)}), bf16[2,64,7,512]{3,0,2,1:T(2,128)(2,1)S(1)}, u32[]{:S(2)}, u32[]{:S(2)}) async-start(bf16[2,64,7,512]{3,0,2,1:T(2,128)(2,1)} %fusion.15), calls=%async_computation.1 | async-start | bytes 1835008 | tf_op jit(solution)/shard_map/all_to_all | solution.py:77
  185.8 79.1 %all-gather.19.cloned.1.call-start = ((), (), s32[]{:S(2)}) async-start(), calls=%async_computation.4 | async-start | bytes 1179648 | tf_op jit(solution)/shard_map/all_gather | solution.py:40
  186.5 39.8 %copy-start.3 = (bf16[512,256]{1,0:T(8,128)(2,1)S(1)}, bf16[512,256]{1,0:T(8,128)(2,1)}, u32[]{:S(2)}) copy-start(bf16[512,256]{1,0:T(8,128)(2,1)} %param.17) | copy-start | bytes 786436
  227.2 61.1 %all-gather.23.cloned.1.call-start = ((), (), s32[]{:S(2)}) async-start(), calls=%async_computation.6 | async-start | bytes 1179648 | tf_op jit(solution)/shard_map/all_gather | solution.py:40
  264.8 163.3 %all-reduce.7.cloned.1.call-start = ((), (), s32[]{:S(2)}) async-start(), calls=%async_computation.8 | async-start | bytes 2097152 | tf_op jit(solution)/shard_map/psum | solution.py:34
  288.3 2.5 copy-start.6
  290.8 270.3 %all-gather.15.cloned.1.call-start = ((), (), s32[]{:S(2)}) async-start(), calls=%async_computation.2 | async-start | bytes 4456448 | tf_op jit(solution)/shard_map/all_gather | solution.py:13
  291.0 138.7 %copy-start.2 = (bf16[1,128,512]{1,2,0:T(8,128)(2,1)}, bf16[1,128,512]{1,2,0:T(8,128)(2,1)S(1)}, u32[]{:S(2)}) copy-start(bf16[1,128,512]{1,2,0:T(8,128)(2,1)S(1)} %copy.153) | copy-start | bytes 393220
  429.4 1.6 copy-start.5
  430.9 164.2 %all-gather.17.cloned.1.call-start = ((), (), s32[]{:S(2)}) async-start(), calls=%async_computation.3 | async-start | bytes 4456448 | tf_op jit(solution)/shard_map/all_gather | solution.py:13
  436.1 193.8 %all-gather.21.cloned.1.call-start = ((), (), s32[]{:S(2)}) async-start(), calls=%async_computation.5 | async-start | bytes 1179648 | tf_op jit(solution)/shard_map/all_gather | solution.py:40
  468.9 92.1 %copy-start.9 = (bf16[4096,8]{0,1:T(8,128)(2,1)}, bf16[4096,8]{0,1:T(8,128)(2,1)S(1)}, u32[]{:S(2)}) copy-start(bf16[4096,8]{0,1:T(8,128)(2,1)S(1)} %all-gather.1) | copy-start | bytes 196612
  499.1 63.2 %copy-start.10 = (bf16[4096,8]{0,1:T(8,128)(2,1)}, bf16[4096,8]{0,1:T(8,128)(2,1)S(1)}, u32[]{:S(2)}) copy-start(bf16[4096,8]{0,1:T(8,128)(2,1)S(1)} %all-gather.2) | copy-start | bytes 196612
  530.8 31.4 %copy-start.8 = (bf16[4096,8]{0,1:T(8,128)(2,1)}, bf16[4096,8]{0,1:T(8,128)(2,1)S(1)}, u32[]{:S(2)}) copy-start(bf16[4096,8]{0,1:T(8,128)(2,1)S(1)} %all-gather.5) | copy-start | bytes 196612
  562.3 31.8 %copy-start.4 = (bf16[512,256]{1,0:T(8,128)(2,1)S(1)}, bf16[512,256]{1,0:T(8,128)(2,1)}, u32[]{:S(2)}) copy-start(bf16[512,256]{1,0:T(8,128)(2,1)} %param.19) | copy-start | bytes 786436
  595.0 57.9 %all-gather.25.cloned.1.call-start = ((), (), s32[]{:S(2)}) async-start(), calls=%async_computation.7 | async-start | bytes 1179648 | tf_op jit(solution)/shard_map/all_gather | solution.py:40
Sparse Core Ops, SparseCore 0:
  12.7 159.0 all-reduce.8
  227.3 23.6 all-gather.18
  264.9 23.3 all-gather.22
  291.4 136.6 all-reduce.6
  431.0 74.3 all-gather.14
  507.2 74.4 all-gather.16
  595.2 23.9 all-gather.20
  628.9 23.9 all-gather.24
